TPU v7x, 32 devices: a whole 2x2x4 slice. The times are simulated.
32 devices in a mesh: dp: 2 (over y), proto: 16 (over z, x, core).
Axes of the slice: x: 2, y: 2, z: 4, core: 2. Of those that a mesh axis runs over, the one named last changes fastest.
Arguments:
- teacher_rows: bfloat16 [128, 256], P(('dp', 'proto')), may hold values from -16 to 16
- student_rows: bfloat16 [128, 256], P(('dp', 'proto')), may hold values from -16 to 16
- teacher_protos: bfloat16 [131072, 256], P(('dp', 'proto')), may hold values from -0.5 to 0.5
- student_protos: bfloat16 [131072, 256], P(('dp', 'proto')), may hold values from -0.5 to 0.5
Outputs:
- row_loss: float32 [128], P(('dp', 'proto'))
- student_grad: float32 [128, 256], P(('dp', 'proto'))
- proto_grad: float32 [131072, 256], P(('dp', 'proto'))
All inputs are finite; a program needn't handle non-finite values.
Results may differ from a plain program's by a relative error of at most 0.0008.
The roundings to bfloat16 on the way count: a program that leaves them out, or rounds other values in their place, can miss the bound.
Values may be sent and summed in bfloat16 or wider, within the bound.
A program may use at most 64 MiB of HBM per device.

v0:
```python
import math

import jax
import jax.numpy as jnp
from jax import lax
from jax.sharding import PartitionSpec as P

BALANCE_ROUNDS = 2


TEACH_TEMP = 0.04
STUD_TEMP = 0.1
LOSS_SCALE = 4096.0
EPSILON = 1e-06


def unit_rows(value_entries):
    widened = value_entries.astype(jnp.float32)
    return widened * lax.rsqrt(jnp.sum(widened * widened, axis=-1, keepdims=True) + EPSILON)


def unit_back(value_entries, cotangent):
    widened = value_entries.astype(jnp.float32)
    inverse = lax.rsqrt(jnp.sum(widened * widened, axis=-1, keepdims=True) + EPSILON)
    projected = jnp.sum(widened * cotangent, axis=-1, keepdims=True)
    return inverse * cotangent - widened * (inverse * inverse * inverse) * projected


def head_core(t_all, s_all, teach_protos, stud_protos, column_total, row_total):
    row_count, feat_width = t_all.shape
    column_number = teach_protos.shape[0]
    step_rows = math.gcd(row_count, max(1, 131072 // column_number))
    blocks = row_count // step_rows
    teach_blocks = t_all.reshape(blocks, step_rows, feat_width)
    stud_blocks = s_all.reshape(blocks, step_rows, feat_width)

    def teacher_exponent(row_block):
        return jnp.exp(
            jnp.einsum("rb,cb->rc", row_block, teach_protos, preferred_element_type=jnp.float32)
            / TEACH_TEMP
        )

    def stud_logits(row_block):
        return (
            jnp.einsum("rb,cb->rc", row_block, stud_protos, preferred_element_type=jnp.float32)
            / STUD_TEMP
        )

    def exp_block(row_block):
        return jnp.sum(jnp.exp(stud_logits(row_block)), axis=1)

    exp_total = row_total(lax.map(exp_block, stud_blocks))
    row_scale = jnp.ones((blocks, step_rows), jnp.float32)
    for balance_round_index in range(BALANCE_ROUNDS):

        def add_columns(running, inputs):
            row_block, weights = inputs
            return (running + jnp.sum(teacher_exponent(row_block) * weights[:, None], axis=0), None)

        col_part, unused = lax.scan(
            add_columns, jnp.zeros((column_number,), jnp.float32), (teach_blocks, row_scale)
        )
        col_scale = 1.0 / column_total(col_part)

        def one_sum(row_block):
            return jnp.sum(teacher_exponent(row_block) * col_scale[None, :], axis=1)

        row_scale = 1.0 / row_total(lax.map(one_sum, teach_blocks))

    def final_block(running, inputs):
        teach_block, stud_block, weights, exp_sums = inputs
        targets = weights[:, None] * teacher_exponent(teach_block) * col_scale[None, :]
        logits = stud_logits(stud_block)
        gradient = (
            LOSS_SCALE * (jnp.exp(logits) / exp_sums[:, None] - targets) / STUD_TEMP
        ).astype(jnp.bfloat16)
        running = running + jnp.einsum(
            "rc,rb->cb", gradient, stud_block, preferred_element_type=jnp.float32
        )
        row_part = jnp.dot(gradient, stud_protos, preferred_element_type=jnp.float32)
        return (running, (row_part, jnp.sum(targets * logits, axis=1)))

    proto_part, (row_parts, dot_parts) = lax.scan(
        final_block,
        jnp.zeros((column_number, feat_width), jnp.float32),
        (teach_blocks, stud_blocks, row_scale, exp_total),
    )
    target_dot = row_total(dot_parts)
    row_loss = (jnp.log(exp_total) - target_dot).reshape(row_count)
    return (row_loss, row_parts.reshape(row_count, feat_width), proto_part)


def body(teacher_rows, student_rows, teacher_protos, student_protos):
    own_rows = teacher_rows.shape[0]
    t_unit = unit_rows(teacher_rows).astype(jnp.bfloat16)
    s_unit = unit_rows(student_rows).astype(jnp.bfloat16)
    tw_own = unit_rows(teacher_protos).astype(jnp.bfloat16)
    sw_own = unit_rows(student_protos).astype(jnp.bfloat16)
    t_all, s_all = (
        lax.all_gather(t_unit, ("dp", "proto"), axis=0, tiled=True),
        lax.all_gather(s_unit, ("dp", "proto"), axis=0, tiled=True),
    )

    def column_total(value_entries):
        return value_entries

    def row_total(value_entries):
        return lax.psum(value_entries, ("dp", "proto"))

    row_loss, row_part, proto_part = head_core(
        t_all, s_all, tw_own, sw_own, column_total, row_total
    )
    row_cot = lax.psum_scatter(row_part, ("dp", "proto"), scatter_dimension=0, tiled=True)
    offset = (lax.axis_index("dp") * lax.axis_size("proto") + lax.axis_index("proto")) * own_rows
    own_loss = lax.dynamic_slice_in_dim(row_loss, offset, own_rows)
    return (own_loss, unit_back(student_rows, row_cot), unit_back(student_protos, proto_part))


def solution(mesh):
    return jax.shard_map(
        body,
        mesh=mesh,
        in_specs=(
            P(("dp", "proto"), None),
            P(("dp", "proto"), None),
            P(("dp", "proto"), None),
            P(("dp", "proto"), None),
        ),
        out_specs=(P(("dp", "proto")), P(("dp", "proto"), None), P(("dp", "proto"), None)),
        check_vma=False,
    )
```

profile of v0, /device:TPU:0, one launch (start us, length us, event | category | flops | bytes accessed | tf_op | source)
XLA Modules:
  0.0 363.9 jit_solution(8439463807403516270)
XLA Ops:
  7.3 2.3 fusion.45
  10.5 43.4 %all-gather.1 = bf16[32,4,256]{2,1,0:T(4,128)(2,1)S(1)} all-gather(bf16[1,4,256]{2,1,0:T(4,128)(2,1)S(1)} %fusion.58), channel_id=1, replica_groups=mesh['dp'=2,'proto'=16] {'dp','proto'}, dimensions={0}, use_global_device_ids=true | all-gather | bytes 67584 | tf_op jit(solution)/shard_map/all_gather | solution.py:100
  53.9 3.8 %fusion.44 = (bf16[4096,256]{1,0:T(8,128)(2,1)S(1)}, bf16[4096,256]{1,0:T(8,128)(2,1)}) fusion(bf16[4096,256]{1,0:T(8,128)(2,1)} %param.18, f32[4096]{0:T(1024)S(1)} %add_rsqrt_fusion, f32[4096]{0:T(1024)S(1)} %get-tuple-element.419, bf16[4096,256]{1,0:T(8,128)(2,1)} %param.19), kind=kLoop, calls=%fused_computation.66 | loop fusion | flops 6291456 | bytes 8421376 | tf_op jit(solution)/shard_map/convert_element_type | solution.py:97
  57.7 3.1 while.72
  60.8 3.5 while.70
  64.4 36.9 %psum.29 = f32[4,32]{1,0:T(4,128)S(1)} all-reduce(f32[4,32]{1,0:T(4,128)S(1)} %get-tuple-element.269), channel_id=1, replica_groups=mesh['dp'=2,'proto'=16] {'dp','proto'}, use_global_device_ids=true, to_apply=%region_14.15 | all-reduce | flops 128 | bytes 1024 | tf_op jit(solution)/shard_map/psum | solution.py:108
  101.3 3.2 while.73
  104.5 3.5 while.71
  108.2 40.4 %all-gather = bf16[32,4,256]{2,1,0:T(4,128)(2,1)S(1)} all-gather(bf16[1,4,256]{2,1,0:T(4,128)(2,1)S(1)} %fusion.57), channel_id=1, replica_groups=mesh['dp'=2,'proto'=16] {'dp','proto'}, dimensions={0}, use_global_device_ids=true | all-gather | bytes 67584 | tf_op jit(solution)/shard_map/all_gather | solution.py:101
  148.7 9.9 %while.69 = (s32[]{:T(128)}, f32[4,32]{1,0:T(4,128)S(1)}, bf16[4,32,256]{2,1,0:T(8,128)(2,1)S(1)}, bf16[4096,256]{1,0:T(8,128)(2,1)}, s32[]{:T(128)}, /*index=5*/s32[]{:T(128)}) while((s32[]{:T(128)}, f32[4,32]{1,0:T(4,128)S(1)}, bf16[4,32,256]{2,1,0:T(8,128)(2,1)S(1)}, bf16[4096,256]{1,0:T(8,128)(2,1)}, s32[]{:T(128)}, ...), condition=%wide.region_4.5_spmd, body=%wide.region_2.4_spmd.sunk | while | flops 67370976 | bytes 2113997 | solution.py:52
  148.7 2.4 fusion.95
  151.2 2.4 fusion.95
  153.6 2.4 fusion.95
  156.1 2.4 fusion.95
  158.6 36.9 %all-reduce.1 = (f32[4,32]{1,0:T(4,128)S(1)}, f32[4,32]{1,0:T(4,128)S(1)}) all-reduce(f32[4,32]{1,0:T(4,128)S(1)} %get-tuple-element.267, f32[4,32]{1,0:T(4,128)S(1)} %get-tuple-element.271), channel_id=1, replica_groups=mesh['dp'=2,'proto'=16] {'dp','proto'}, use_global_device_ids=true, to_apply=%region_5.0 | all-reduce | flops 256 | bytes 2048 | tf_op jit(solution)/shard_map/psum | solution.py:108
  195.5 35.3 %while.74 = (s32[]{:T(128)}, f32[4096,256]{1,0:T(8,128)}, f32[4,32,256]{2,1,0:T(8,128)}, f32[4,32]{1,0:T(4,128)S(1)}, bf16[4,32,256]{2,1,0:T(8,128)(2,1)S(1)}, /...) while((s32[]{:T(128)}, f32[4096,256]{1,0:T(8,128)}, ...), condition=%wide.region_24.25_spmd.clone, body=%wide.region_22.24_spmd.clone.sunk | while | flops 271843296 | bytes 25004600 | solution.py:83
  195.5 2.3 convolution_multiply_fusion.8
  198.7 2.8 convolution_add_fusion.2
  201.5 1.1 fusion.116
  202.6 2.3 convolution_multiply_fusion.8
  205.8 5.1 %convolution_add_fusion.2 = f32[4096,256]{1,0:T(8,128)} fusion(bf16[32,4096]{1,0:T(8,128)(2,1)S(1)} %get-tuple-element.640, f32[4096,256]{1,0:T(8,128)} %get-tuple-element.755, pred[]{:T(512)S(6)} %compare.11, bf16[4,32,256]{2,1,0:T(8,128)(2,1)S(1)} %get-tuple-element.771, s32[]{:T(128)} %get-tuple-element.754), kind=kOutput, calls=%fused_computation.36.clone.1 | convolution fusion | flops 69206016 | bytes 8667141 | tf_op jit(solution)/shard_map/while/body/eval_jaxpr/rc,rb->cb/dot_general | solution.py:77
  210.9 1.1 fusion.116
  212.0 2.3 convolution_multiply_fusion.8
  215.2 5.1 %convolution_add_fusion.2 = f32[4096,256]{1,0:T(8,128)} fusion(bf16[32,4096]{1,0:T(8,128)(2,1)S(1)} %get-tuple-element.640, f32[4096,256]{1,0:T(8,128)} %get-tuple-element.755, pred[]{:T(512)S(6)} %compare.11, bf16[4,32,256]{2,1,0:T(8,128)(2,1)S(1)} %get-tuple-element.771, s32[]{:T(128)} %get-tuple-element.754), kind=kOutput, calls=%fused_computation.36.clone.1 | convolution fusion | flops 69206016 | bytes 8667141 | tf_op jit(solution)/shard_map/while/body/eval_jaxpr/rc,rb->cb/dot_general | solution.py:77
  220.3 1.1 fusion.116
  221.4 2.3 convolution_multiply_fusion.8
  224.6 5.1 %convolution_add_fusion.2 = f32[4096,256]{1,0:T(8,128)} fusion(bf16[32,4096]{1,0:T(8,128)(2,1)S(1)} %get-tuple-element.640, f32[4096,256]{1,0:T(8,128)} %get-tuple-element.755, pred[]{:T(512)S(6)} %compare.11, bf16[4,32,256]{2,1,0:T(8,128)(2,1)S(1)} %get-tuple-element.771, s32[]{:T(128)} %get-tuple-element.754), kind=kOutput, calls=%fused_computation.36.clone.1 | convolution fusion | flops 69206016 | bytes 8667141 | tf_op jit(solution)/shard_map/while/body/eval_jaxpr/rc,rb->cb/dot_general | solution.py:77
  230.9 3.6 fusion.49
  234.5 42.4 %psum.31 = f32[4,32]{1,0:T(4,128)S(1)} all-reduce(f32[4,32]{1,0:T(4,128)S(1)} %get-tuple-element.272), channel_id=1, replica_groups=mesh['dp'=2,'proto'=16] {'dp','proto'}, use_global_device_ids=true, to_apply=%region_25.26 | all-reduce | flops 128 | bytes 1024 | tf_op jit(solution)/shard_map/psum | solution.py:108
  276.9 5.6 %fusion.48 = f32[4096,256]{1,0:T(8,128)} fusion(bf16[4096,256]{1,0:T(8,128)(2,1)S(1)} %copy-done.1, f32[4096,256]{1,0:T(8,128)} %get-tuple-element.274, f32[4096]{0:T(1024)S(1)} %fusion.49, f32[4096]{0:T(1024)S(1)} %get-tuple-element.418, f32[4096]{0:T(1024)S(1)} %get-tuple-element.419), kind=kLoop, calls=%fused_computation.70 | loop fusion | flops 5242880 | bytes 10534912 | tf_op jit(solution)/shard_map/sub | solution.py:26
  283.2 71.7 %all-reduce.4.cloned.1.call-done = f32[128,256]{1,0:T(8,128)} async-done(((f32[128,256]{1,0:T(8,128)}), f32[128,256]{1,0:T(8,128)}) %all-reduce.4.cloned.1.call-update) | async-done | bytes 131088
  355.7 1.4 fusion.55
  (98 shorter events, 20.6 us)
Async XLA Ops:
  7.2 2.5 copy-start.2
  7.2 347.7 %all-reduce.4.cloned.1.call-start = ((), (), s32[]{:S(2)}) async-start(), calls=%async_computation | async-start | bytes 262144
  7.3 3.0 copy-start.4
  104.5 3.6 copy-start.3
  198.7 2.8 copy-start
  205.8 5.1 %copy-start = (bf16[4096,256]{1,0:T(8,128)(2,1)S(1)}, bf16[4096,256]{1,0:T(8,128)(2,1)}, u32[]{:S(2)}) copy-start(bf16[4096,256]{1,0:T(8,128)(2,1)} %get-tuple-element.772) | copy-start | bytes 6291460 | tf_op jit(solution)/shard_map/while
  215.2 5.1 %copy-start = (bf16[4096,256]{1,0:T(8,128)(2,1)S(1)}, bf16[4096,256]{1,0:T(8,128)(2,1)}, u32[]{:S(2)}) copy-start(bf16[4096,256]{1,0:T(8,128)(2,1)} %get-tuple-element.772) | copy-start | bytes 6291460 | tf_op jit(solution)/shard_map/while
  224.6 5.1 %copy-start = (bf16[4096,256]{1,0:T(8,128)(2,1)S(1)}, bf16[4096,256]{1,0:T(8,128)(2,1)}, u32[]{:S(2)}) copy-start(bf16[4096,256]{1,0:T(8,128)(2,1)} %get-tuple-element.772) | copy-start | bytes 6291460 | tf_op jit(solution)/shard_map/while
  230.8 46.0 %copy-start.1 = (bf16[4096,256]{1,0:T(8,128)(2,1)S(1)}, bf16[4096,256]{1,0:T(8,128)(2,1)}, u32[]{:S(2)}) copy-start(bf16[4096,256]{1,0:T(8,128)(2,1)} %param.19) | copy-start | bytes 6291460
Sparse Core Ops, SparseCore 0:
  231.0 123.8 all-reduce.3
where the time goes:
time: 365 us; the launch traced here: 364 us
  blocking collectives  200 us (55%)
  waiting for transfers between devices  71.7 us (20%)
  matrix products  57.4 us (16%)
  other arithmetic  18.7 us (5%)
  between operations  14.2 us (4%)
    psum x3, blocking collectives, row_total(): return lax.psum(value_entries, ('dp', 'proto'))  116 us
    unnamed x2, waiting for transfers between devices  71.7 us
    all_gather x1, blocking collectives, body(): lax.all_gather(t_unit, ('dp', 'proto'), axis=0, tiled=True)  43.4 us
    all_gather x1, blocking collectives, body(): lax.all_gather(s_unit, ('dp', 'proto'), axis=0, tiled=True)  40.4 us
    dot_general x8, matrix products, stud_logits(): jnp.einsum('rb,cb->rc', row_block, stud_protos, preferred_element_type=jn...  18.9 us
    dot_general x4, matrix products, final_block(): jnp.einsum('rc,rb->cb', gradient, stud_block, preferred_element_type=jnp....  18.1 us
    dot_general x20, matrix products, teacher_exponent(): jnp.einsum('rb,cb->rc', row_block, teach_protos, preferred_element_type=j...  16.1 us
  transfers between devices with their start and end apart: 1, of which 1 were waited for; matrix products, arithmetic and copies ran while one was open for 3% of the time, Pallas kernels for 0%

commit v1 on v0

v1 whole, which is shorter than its diff:
```python
import functools

import jax
import jax.numpy as jnp
from jax import lax
from jax.experimental import pallas as pl
from jax.experimental.pallas import tpu as pltpu
from jax.sharding import PartitionSpec as P

TEACH_TEMP = 0.04
STUD_TEMP = 0.1
LOSS_SCALE = 4096.0
EPSILON = 1e-06
AXES = ("dp", "proto")
LANES = 128
LOAD_PARTS = 4


def inverse_norm(x):
    return lax.rsqrt(jnp.sum(x * x, axis=-1, keepdims=True) + EPSILON)


def fold_lanes(x):
    total = x[:, :LANES]
    for start in range(LANES, x.shape[1], LANES):
        total = total + x[:, start:start + LANES]
    return total


def eye():
    shape = (LANES, LANES)
    return lax.broadcasted_iota(jnp.int32, shape, 0) == lax.broadcasted_iota(jnp.int32, shape, 1)


def to_lanes(column):
    blocks = [
        jnp.sum(jnp.where(eye(), column[i:i + LANES], 0.0), axis=0, keepdims=True)
        for i in range(0, column.shape[0], LANES)
    ]
    return blocks[0] if len(blocks) == 1 else jnp.concatenate(blocks, axis=1)


def to_column(row):
    blocks = [
        jnp.sum(jnp.where(eye(), row[:, i:i + LANES], 0.0), axis=1, keepdims=True)
        for i in range(0, row.shape[1], LANES)
    ]
    return blocks[0] if len(blocks) == 1 else jnp.concatenate(blocks, axis=0)


def kernel(
    dp, proto, cols,
    t_ref, s_ref, tw_hbm, sw_hbm,
    loss_ref, sgrad_ref, pgrad_ref,
    tw_raw, sw_raw, tw_unit, sw_unit, sw_inv, texp, logit, delta,
    rows_buf, sums1, sums2, part, landed, t_all, s_all, col_ref,
    load_sem, send_sem, recv_sem,
):
    n = dp * proto
    own = t_ref.shape[0]
    total_rows = n * own
    width = t_ref.shape[1]
    count = tw_raw.shape[0]
    chunks = count // cols
    me = lax.axis_index("dp") * proto + lax.axis_index("proto")

    def coords(j):
        peer = lax.rem(me + j, n)
        return peer, (lax.div(peer, proto), lax.rem(peer, proto))

    piece = count // LOAD_PARTS
    loads = []
    for k in range(LOAD_PARTS):
        for index, (hbm, raw) in enumerate(((tw_hbm, tw_raw), (sw_hbm, sw_raw))):
            span = pl.ds(k * piece, piece)
            copy = pltpu.make_async_copy(hbm.at[span], raw.at[span], load_sem.at[index, k])
            copy.start()
            loads.append(copy)

    barrier = pltpu.get_barrier_semaphore()

    @pl.loop(1, n)
    def _(j):
        pl.semaphore_signal(barrier, inc=1, device_id=coords(j)[1], device_id_type=pl.DeviceIdType.MESH)

    t_own = t_ref[...].astype(jnp.float32)
    s_own = s_ref[...].astype(jnp.float32)
    s_own_inv = inverse_norm(s_own)
    t_rounded = (t_own * inverse_norm(t_own)).astype(jnp.bfloat16).astype(jnp.float32)
    s_rounded = (s_own * s_own_inv).astype(jnp.bfloat16).astype(jnp.float32)
    rows_buf[me] = jnp.concatenate([t_rounded, s_rounded], axis=0)
    pl.semaphore_wait(barrier, n - 1)

    def spread(phase, source, target):
        @pl.loop(1, n)
        def _(j):
            peer, device = coords(j)
            pltpu.make_async_remote_copy(
                src_ref=source(peer), dst_ref=target.at[me],
                send_sem=send_sem.at[phase], recv_sem=recv_sem.at[phase],
                device_id=device, device_id_type=pl.DeviceIdType.MESH,
            ).start()

    def whole(phase, target):
        span = pl.ds(0, n - 1)
        return pltpu.make_async_remote_copy(
            src_ref=target.at[span], dst_ref=target.at[span],
            send_sem=send_sem.at[phase], recv_sem=recv_sem.at[phase],
            device_id=coords(1)[1], device_id_type=pl.DeviceIdType.MESH,
        )

    spread(0, lambda peer: rows_buf.at[me], rows_buf)

    norm_rows = min(piece, 256)
    for k in range(LOAD_PARTS):
        for index, raw in enumerate((tw_raw, sw_raw)):
            loads[2 * k + index].wait()

            @pl.loop(0, piece // norm_rows)
            def _(c, k=k, index=index, raw=raw):
                span = pl.ds(pl.multiple_of(k * piece + c * norm_rows, norm_rows), norm_rows)
                x = raw[span].astype(jnp.float32)
                inverse = inverse_norm(x)
                unit = (x * inverse).astype(jnp.bfloat16)
                if index == 0:
                    tw_unit[span] = unit
                else:
                    sw_unit[span] = unit
                    sw_inv[span] = jnp.broadcast_to(inverse, (norm_rows, LANES))

    whole(0, rows_buf).wait_recv()
    paired = rows_buf[...].reshape(n // 2, 2, 2 * own, width)
    first, second = paired[:, 0], paired[:, 1]
    upper = lax.broadcasted_iota(jnp.int32, first.shape, 1) < own
    t_all[...] = jnp.where(upper, first, pltpu.roll(second, own, 1)).reshape(total_rows, width).astype(jnp.bfloat16)
    s_all[...] = jnp.where(upper, pltpu.roll(first, own, 1), second).reshape(total_rows, width).astype(jnp.bfloat16)

    transposed = (((1,), (1,)), ((), ()))
    zeros = jnp.zeros((total_rows, LANES), jnp.float32)

    def span_of(c):
        return pl.ds(pl.multiple_of(c * cols, cols), cols)

    def first_pass(c, carry):
        row_sum, exp_sum = carry
        span = span_of(c)
        expo = jnp.exp(
            lax.dot_general(t_all[...], tw_unit[span], transposed, preferred_element_type=jnp.float32)
            * (1.0 / TEACH_TEMP)
        )
        texp[:, span] = expo
        scale = 1.0 / jnp.sum(expo, axis=0, keepdims=True)
        row_sum = row_sum + fold_lanes(expo * scale)
        logits = lax.dot_general(
            s_all[...], sw_unit[span], transposed, preferred_element_type=jnp.float32
        ) * (1.0 / STUD_TEMP)
        logit[:, span] = logits
        exp_sum = exp_sum + fold_lanes(jnp.exp(logits))
        return row_sum, exp_sum

    def share(phase, sums, one, two):
        sums[me] = jnp.concatenate(
            [to_lanes(jnp.sum(x, axis=1, keepdims=True)) for x in (one, two)], axis=0
        )
        spread(phase, lambda peer: sums.at[me], sums)
        whole(phase, sums).wait_recv()
        total = jnp.sum(sums[...], axis=0)
        return total[0:1], total[1:2]

    row_sum, exp_sum = lax.fori_loop(0, chunks, first_pass, (zeros, zeros))
    row_total, exp_total = share(1, sums1, row_sum, exp_sum)
    row_scale = to_column(1.0 / row_total)

    def second_pass(c, carry):
        row_sum, dot_sum = carry
        span = span_of(c)
        expo = texp[:, span]
        scale = 1.0 / jnp.sum(expo * row_scale, axis=0, keepdims=True)
        scaled = expo * scale
        texp[:, span] = scaled
        return row_sum + fold_lanes(scaled), dot_sum + fold_lanes(scaled * logit[:, span])

    row_sum, dot_sum = lax.fori_loop(0, chunks, second_pass, (zeros, zeros))
    row_total, dot_total = share(2, sums2, row_sum, dot_sum)
    factor = LOSS_SCALE / STUD_TEMP
    row_scale = to_column(factor / row_total)
    exp_scale = to_column(factor / exp_total)

    def third_pass(c, carry):
        span = span_of(c)
        gradient = (jnp.exp(logit[:, span]) * exp_scale - texp[:, span] * row_scale).astype(jnp.bfloat16)
        delta[:, span] = gradient
        return carry + jnp.dot(gradient, sw_unit[span], preferred_element_type=jnp.float32)

    row_part = lax.fori_loop(0, chunks, third_pass, jnp.zeros((total_rows, width), jnp.float32))
    part[...] = row_part.reshape(n, own, width)
    landed[me] = part[me]
    spread(3, lambda peer: part.at[peer], landed)

    loss = jnp.log(exp_total) - dot_total / row_total
    shape = (total_rows, LANES)
    mine = lax.broadcasted_iota(jnp.int32, shape, 0) == me * own + lax.broadcasted_iota(jnp.int32, shape, 1)
    loss_ref[...] = jnp.sum(jnp.where(mine, to_column(loss), 0.0), axis=0, keepdims=True)[:, :own]

    @pl.loop(0, chunks)
    def _(c):
        span = span_of(c)
        g = lax.dot_general(
            delta[:, span], s_all[...], (((0,), (0,)), ((), ())), preferred_element_type=jnp.float32
        )
        x = sw_raw[span].astype(jnp.float32)
        inverse = jnp.concatenate([sw_inv[span]] * (width // LANES), axis=1)
        projected = jnp.sum(x * g, axis=1, keepdims=True)
        pgrad_ref[span] = inverse * g - x * ((inverse * inverse * inverse) * projected)

    whole(3, landed).wait_recv()
    g = jnp.sum(landed[...], axis=0)
    projected = jnp.sum(s_own * g, axis=1, keepdims=True)
    sgrad_ref[...] = s_own_inv * g - s_own * (s_own_inv * s_own_inv * s_own_inv) * projected
    for phase, target in enumerate((rows_buf, sums1, sums2, landed)):
        whole(phase, target).wait_send()


def body(dp, proto, teacher_rows, student_rows, teacher_protos, student_protos):
    n = dp * proto
    own, width = teacher_rows.shape
    count = teacher_protos.shape[0]
    rows = n * own
    cols = min(count, max(LANES, 32768 // rows))
    f32, bf16 = jnp.float32, jnp.bfloat16
    vmem = pl.BlockSpec(memory_space=pltpu.VMEM)
    hbm = pl.BlockSpec(memory_space=pl.ANY)
    loss, sgrad, pgrad = pl.pallas_call(
        functools.partial(kernel, dp, proto, cols),
        out_shape=(
            jax.ShapeDtypeStruct((1, own), f32),
            jax.ShapeDtypeStruct((own, width), f32),
            jax.ShapeDtypeStruct((count, width), f32),
        ),
        in_specs=[vmem, vmem, hbm, hbm],
        out_specs=(vmem, vmem, vmem),
        scratch_shapes=[
            pltpu.VMEM((count, width), bf16),
            pltpu.VMEM((count, width), bf16),
            pltpu.VMEM((count, width), bf16),
            pltpu.VMEM((count, width), bf16),
            pltpu.VMEM((count, LANES), f32),
            pltpu.VMEM((rows, count), f32),
            pltpu.VMEM((rows, count), f32),
            pltpu.VMEM((rows, count), bf16),
            pltpu.VMEM((n, 2 * own, width), f32),
            pltpu.VMEM((n, 2, rows), f32),
            pltpu.VMEM((n, 2, rows), f32),
            pltpu.VMEM((n, own, width), f32),
            pltpu.VMEM((n, own, width), f32),
            pltpu.VMEM((rows, width), bf16),
            pltpu.VMEM((rows, width), bf16),
            pltpu.VMEM((1, count), f32),
            pltpu.SemaphoreType.DMA((2, LOAD_PARTS)),
            pltpu.SemaphoreType.DMA((4,)),
            pltpu.SemaphoreType.DMA((4,)),
        ],
        compiler_params=pltpu.CompilerParams(
            collective_id=0, has_side_effects=True, vmem_limit_bytes=56 * 1024 * 1024
        ),
    )(teacher_rows, student_rows, teacher_protos, student_protos)
    return loss.reshape(own), sgrad, pgrad


def solution(mesh):
    spec = P(AXES, None)
    return jax.shard_map(
        functools.partial(body, mesh.shape["dp"], mesh.shape["proto"]),
        mesh=mesh,
        in_specs=(spec,) * 4,
        out_specs=(P(AXES), spec, spec),
        check_vma=False,
    )
```

time: 365 us -> 48.4 us (0.13)
  blocking collectives: 200 us -> 0 us
  waiting for transfers between devices: 71.7 us -> 0 us
  matrix products: 57.4 us -> 0 us
  Pallas kernels: 0 us -> 40.6 us
  other arithmetic: 18.7 us -> 0 us
  between operations: 14.2 us -> 0.64 us
  local copies, waits for them, and re-layouts: 1.47 us -> 6.92 us
    psum x3 -> x0, blocking collectives: 116 us -> none  [row_total(): return lax.psum(value_entries, ('dp', 'proto'))]
    all_gather x2 -> x0, blocking collectives: 83.8 us -> none  [the longest x1 43.4 us: body(): lax.all_gather(t_unit, ('dp', 'proto'), axis=0, tiled=True)]
    unnamed x2 -> x0, waiting for transfers between devices: 71.7 us -> none
    dot_general x36 -> x0, matrix products: 57.4 us -> none  [the longest x8 18.9 us: stud_logits(): jnp.einsum('rb,cb->rc', row_block, stud_protos, preferred_element_type=jn...]
    pallas_call x0 -> x1, Pallas kernels: none -> 40.6 us  [body(): pl.pallas_call(functools.partial(kernel, dp, proto, cols), out_shape=(jax...]
    reduce_sum x6 -> x0, other arithmetic: 7.62 us -> none  [the longest x2 4.43 us: unit_back(): projected = jnp.sum(widened * cotangent, axis=-1, keepdims=True)]
    sub x3 -> x0, other arithmetic: 6.99 us -> none  [the longest x2 6.99 us: unit_back(): inverse * cotangent - widened * (inverse * inverse * inverse) * projected]
    unnamed x8 -> x3, local copies, waits for them, and re-layouts: 0.03 us -> 6.92 us
  transfers between devices with their start and end apart: 1 -> 0, of which waited for: 1 -> 0; matrix products, arithmetic and copies ran while one was open for 3% -> 0% of each run, Pallas kernels for 0% -> 0%
where the time goes in v1:
time: 48.4 us; the launch traced here: 48.1 us
  Pallas kernels  40.6 us (84%)
  local copies, waits for them, and re-layouts  6.92 us (14%)
  between operations  0.64 us (1%)
    pallas_call x1, Pallas kernels, body(): pl.pallas_call(functools.partial(kernel, dp, proto, cols), out_shape=(jax...  40.6 us
    unnamed x3, local copies, waits for them, and re-layouts  6.92 us

profile of v1, /device:TPU:0, one launch (start us, length us, event | category | flops | bytes accessed | tf_op | source)
XLA Modules:
  0.0 48.1 jit_solution(12623321653988068862)
XLA Ops:
  0.6 40.6 %shard_map.67 = (f32[1,4]{1,0:T(1,128)}, f32[4,256]{1,0:T(4,128)}, f32[4096,256]{1,0:T(8,128)}) custom-call(bf16[4,256]{1,0:T(4,128)(2,1)} %t_ref.1, bf16[4,256]{1,0:T(4,128)(2,1)} %s_ref.1, bf16[4096,256]{1,0:T(8,128)(2,1)} %tw_hbm.1, bf16[4096,256]{1,0:T(8,128)(2,1)} %sw_hbm.1), custom_call_target="tpu_custom_call" | custom-call | tf_op jit(solution)/shard_map/pallas_call | solution.py:233
  41.2 1.2 %copy.10 = f32[4]{0:T(128)} copy(f32[4]{0:T(128)} %bitcast.1) | data formatting | bytes 32
  42.4 1.3 %copy.11 = f32[4,256]{1,0:T(4,128)} copy(f32[4,256]{1,0:T(4,128)} %get-tuple-element.13) | data formatting | bytes 8192
  43.7 4.5 %copy.12 = f32[4096,256]{1,0:T(8,128)} copy(f32[4096,256]{1,0:T(8,128)} %get-tuple-element.14) | data formatting | bytes 8388608

commit v2 on v1

--- a/solution.py
+++ b/solution.py
@@ -20,6 +20,19 @@
     return lax.rsqrt(jnp.sum(x * x, axis=-1, keepdims=True) + EPSILON)
 
 
+def sum_wide(x):
+    ones = jnp.ones((x.shape[1], LANES), jnp.bfloat16)
+    high = x.astype(jnp.bfloat16)
+    low = (x - high.astype(jnp.float32)).astype(jnp.bfloat16)
+    return jnp.dot(high, ones, preferred_element_type=jnp.float32) + jnp.dot(
+        low, ones, preferred_element_type=jnp.float32
+    )
+
+
+def widen(x, width):
+    return jnp.concatenate([x] * (width // LANES), axis=1)
+
+
 def fold_lanes(x):
     total = x[:, :LANES]
     for start in range(LANES, x.shape[1], LANES):
@@ -53,7 +66,7 @@
     t_ref, s_ref, tw_hbm, sw_hbm,
     loss_ref, sgrad_ref, pgrad_ref,
     tw_raw, sw_raw, tw_unit, sw_unit, sw_inv, texp, logit, delta,
-    rows_buf, sums1, sums2, part, landed, t_all, s_all, col_ref,
+    rows_buf, sums1, sums2, part, landed, t_all, s_all,
     load_sem, send_sem, recv_sem,
 ):
     n = dp * proto
@@ -111,7 +124,7 @@
 
     spread(0, lambda peer: rows_buf.at[me], rows_buf)
 
-    norm_rows = min(piece, 256)
+    norm_rows = min(piece, 512)
     for k in range(LOAD_PARTS):
         for index, raw in enumerate((tw_raw, sw_raw)):
             loads[2 * k + index].wait()
@@ -120,13 +133,13 @@
             def _(c, k=k, index=index, raw=raw):
                 span = pl.ds(pl.multiple_of(k * piece + c * norm_rows, norm_rows), norm_rows)
                 x = raw[span].astype(jnp.float32)
-                inverse = inverse_norm(x)
-                unit = (x * inverse).astype(jnp.bfloat16)
+                inverse = lax.rsqrt(sum_wide(x * x) + EPSILON)
+                unit = (x * widen(inverse, width)).astype(jnp.bfloat16)
                 if index == 0:
                     tw_unit[span] = unit
                 else:
                     sw_unit[span] = unit
-                    sw_inv[span] = jnp.broadcast_to(inverse, (norm_rows, LANES))
+                    sw_inv[span] = inverse
 
     whole(0, rows_buf).wait_recv()
     paired = rows_buf[...].reshape(n // 2, 2, 2 * own, width)
@@ -209,9 +222,9 @@
             delta[:, span], s_all[...], (((0,), (0,)), ((), ())), preferred_element_type=jnp.float32
         )
         x = sw_raw[span].astype(jnp.float32)
-        inverse = jnp.concatenate([sw_inv[span]] * (width // LANES), axis=1)
-        projected = jnp.sum(x * g, axis=1, keepdims=True)
-        pgrad_ref[span] = inverse * g - x * ((inverse * inverse * inverse) * projected)
+        inverse = sw_inv[span]
+        pull = (inverse * inverse * inverse) * sum_wide(x * g)
+        pgrad_ref[span] = widen(inverse, width) * g - x * widen(pull, width)
 
     whole(3, landed).wait_recv()
     g = jnp.sum(landed[...], axis=0)
@@ -226,7 +239,7 @@
     own, width = teacher_rows.shape
     count = teacher_protos.shape[0]
     rows = n * own
-    cols = min(count, max(LANES, 32768 // rows))
+    cols = min(count, max(LANES, 65536 // rows))
     f32, bf16 = jnp.float32, jnp.bfloat16
     vmem = pl.BlockSpec(memory_space=pltpu.VMEM)
     hbm = pl.BlockSpec(memory_space=pl.ANY)
@@ -235,7 +248,7 @@
         out_shape=(
             jax.ShapeDtypeStruct((1, own), f32),
             jax.ShapeDtypeStruct((own, width), f32),
-            jax.ShapeDtypeStruct((count, width), f32),
+            pltpu.VMEM((count, width), f32),
         ),
         in_specs=[vmem, vmem, hbm, hbm],
         out_specs=(vmem, vmem, vmem),
@@ -255,7 +268,6 @@
             pltpu.VMEM((n, own, width), f32),
             pltpu.VMEM((rows, width), bf16),
             pltpu.VMEM((rows, width), bf16),
-            pltpu.VMEM((1, count), f32),
             pltpu.SemaphoreType.DMA((2, LOAD_PARTS)),
             pltpu.SemaphoreType.DMA((4,)),
             pltpu.SemaphoreType.DMA((4,)),

time: 48.4 us -> 40.2 us (0.83)
  Pallas kernels: 40.6 us -> 36.2 us
  local copies, waits for them, and re-layouts: 6.92 us -> 3.13 us
    pallas_call x1, Pallas kernels: 40.6 us -> 36.2 us  [body(): pl.pallas_call(functools.partial(kernel, dp, proto, cols), out_shape=(jax...]
    unnamed x3 -> x7, local copies, waits for them, and re-layouts: 6.92 us -> 3.13 us
where the time goes in v2:
time: 40.2 us; the launch traced here: 40 us
  Pallas kernels  36.2 us (90%)
  local copies, waits for them, and re-layouts  3.13 us (8%)
  between operations  0.66 us (2%)
    pallas_call x1, Pallas kernels, body(): pl.pallas_call(functools.partial(kernel, dp, proto, cols), out_shape=(jax...  36.2 us
    unnamed x7, local copies, waits for them, and re-layouts  3.13 us

profile of v2, /device:TPU:0, one launch (start us, length us, event | category | flops | bytes accessed | tf_op | source)
XLA Modules:
  0.0 40.0 jit_solution(8223118752408620793)
XLA Ops:
  0.6 36.2 %shard_map.67 = (f32[1,4]{1,0:T(1,128)}, f32[4,256]{1,0:T(4,128)}, f32[4096,256]{1,0:T(8,128)S(1)}) custom-call(bf16[4,256]{1,0:T(4,128)(2,1)} %t_ref.1, bf16[4,256]{1,0:T(4,128)(2,1)} %s_ref.1, bf16[4096,256]{1,0:T(8,128)(2,1)} %tw_hbm.1, bf16[4096,256]{1,0:T(8,128)(2,1)} %sw_hbm.1), custom_call_target="tpu_custom_call" | custom-call | tf_op jit(solution)/shard_map/pallas_call | solution.py:246
  36.9 0.0 copy-start.1
  36.9 0.0 copy-start
  36.9 2.0 %copy.10 = f32[4096,256]{1,0:T(8,128)} copy(f32[4096,256]{1,0:T(8,128)S(1)} %get-tuple-element.11) | data formatting | bytes 8388608
  38.9 0.0 copy-done.1
  38.9 0.5 %copy.11 = f32[4]{0:T(128)} copy(f32[4]{0:T(128)S(1)} %bitcast.1) | data formatting | bytes 32
  39.4 0.0 copy-done
  39.4 0.6 %copy.12 = f32[4,256]{1,0:T(4,128)} copy(f32[4,256]{1,0:T(4,128)S(1)} %copy-done) | data formatting | bytes 8192
Async XLA Ops:
  36.9 2.0 %copy-start.1 = (f32[1,4]{1,0:T(1,128)S(1)}, f32[1,4]{1,0:T(1,128)}, u32[]{:S(2)}) copy-start(f32[1,4]{1,0:T(1,128)} %get-tuple-element.6) | copy-start | bytes 52
  36.9 2.5 %copy-start = (f32[4,256]{1,0:T(4,128)S(1)}, f32[4,256]{1,0:T(4,128)}, u32[]{:S(2)}) copy-start(f32[4,256]{1,0:T(4,128)} %get-tuple-element.16) | copy-start | bytes 12292

commit v3 on v2

--- a/solution.py
+++ b/solution.py
@@ -65,7 +65,7 @@
     dp, proto, cols,
     t_ref, s_ref, tw_hbm, sw_hbm,
     loss_ref, sgrad_ref, pgrad_ref,
-    tw_raw, sw_raw, tw_unit, sw_unit, sw_inv, texp, logit, delta,
+    tw_raw, sw_raw, tw_unit, sw_unit, sw_inv, texp, logit, sexp, delta,
     rows_buf, sums1, sums2, part, landed, t_all, s_all,
     load_sem, send_sem, recv_sem,
 ):
@@ -152,10 +152,14 @@
     zeros = jnp.zeros((total_rows, LANES), jnp.float32)
 
     def span_of(c):
-        return pl.ds(pl.multiple_of(c * cols, cols), cols)
+        return pl.ds(c * cols, cols)
+
+    def over_chunks(step, carry):
+        for c in range(chunks):
+            carry = step(c, carry)
+        return carry
 
     def first_pass(c, carry):
-        row_sum, exp_sum = carry
         span = span_of(c)
         expo = jnp.exp(
             lax.dot_general(t_all[...], tw_unit[span], transposed, preferred_element_type=jnp.float32)
@@ -163,25 +167,30 @@
         )
         texp[:, span] = expo
         scale = 1.0 / jnp.sum(expo, axis=0, keepdims=True)
-        row_sum = row_sum + fold_lanes(expo * scale)
+        return carry + fold_lanes(expo * scale)
+
+    def student_pass(c, carry):
+        span = span_of(c)
         logits = lax.dot_general(
             s_all[...], sw_unit[span], transposed, preferred_element_type=jnp.float32
         ) * (1.0 / STUD_TEMP)
         logit[:, span] = logits
-        exp_sum = exp_sum + fold_lanes(jnp.exp(logits))
-        return row_sum, exp_sum
-
-    def share(phase, sums, one, two):
-        sums[me] = jnp.concatenate(
-            [to_lanes(jnp.sum(x, axis=1, keepdims=True)) for x in (one, two)], axis=0
-        )
+        expo = jnp.exp(logits)
+        sexp[:, span] = expo
+        return carry + fold_lanes(expo)
+
+    def send_sums(phase, sums, parts):
+        rows = [to_lanes(jnp.sum(x, axis=1, keepdims=True)) for x in parts]
+        sums[me] = rows[0] if len(rows) == 1 else jnp.concatenate(rows, axis=0)
         spread(phase, lambda peer: sums.at[me], sums)
+
+    def receive_sums(phase, sums):
         whole(phase, sums).wait_recv()
-        total = jnp.sum(sums[...], axis=0)
-        return total[0:1], total[1:2]
-
-    row_sum, exp_sum = lax.fori_loop(0, chunks, first_pass, (zeros, zeros))
-    row_total, exp_total = share(1, sums1, row_sum, exp_sum)
+        return jnp.sum(sums[...], axis=0)
+
+    send_sums(1, sums1, (over_chunks(first_pass, zeros),))
+    exp_sum = over_chunks(student_pass, zeros)
+    row_total = receive_sums(1, sums1)
     row_scale = to_column(1.0 / row_total)
 
     def second_pass(c, carry):
@@ -193,19 +202,21 @@
         texp[:, span] = scaled
         return row_sum + fold_lanes(scaled), dot_sum + fold_lanes(scaled * logit[:, span])
 
-    row_sum, dot_sum = lax.fori_loop(0, chunks, second_pass, (zeros, zeros))
-    row_total, dot_total = share(2, sums2, row_sum, dot_sum)
+    row_sum, dot_sum = over_chunks(second_pass, (zeros, zeros))
+    send_sums(2, sums2, (row_sum, dot_sum, exp_sum))
+    total = receive_sums(2, sums2)
+    row_total, dot_total, exp_total = total[0:1], total[1:2], total[2:3]
     factor = LOSS_SCALE / STUD_TEMP
     row_scale = to_column(factor / row_total)
     exp_scale = to_column(factor / exp_total)
 
     def third_pass(c, carry):
         span = span_of(c)
-        gradient = (jnp.exp(logit[:, span]) * exp_scale - texp[:, span] * row_scale).astype(jnp.bfloat16)
+        gradient = (sexp[:, span] * exp_scale - texp[:, span] * row_scale).astype(jnp.bfloat16)
         delta[:, span] = gradient
         return carry + jnp.dot(gradient, sw_unit[span], preferred_element_type=jnp.float32)
 
-    row_part = lax.fori_loop(0, chunks, third_pass, jnp.zeros((total_rows, width), jnp.float32))
+    row_part = over_chunks(third_pass, jnp.zeros((total_rows, width), jnp.float32))
     part[...] = row_part.reshape(n, own, width)
     landed[me] = part[me]
     spread(3, lambda peer: part.at[peer], landed)
@@ -215,8 +226,7 @@
     mine = lax.broadcasted_iota(jnp.int32, shape, 0) == me * own + lax.broadcasted_iota(jnp.int32, shape, 1)
     loss_ref[...] = jnp.sum(jnp.where(mine, to_column(loss), 0.0), axis=0, keepdims=True)[:, :own]
 
-    @pl.loop(0, chunks)
-    def _(c):
+    for c in range(chunks):
         span = span_of(c)
         g = lax.dot_general(
             delta[:, span], s_all[...], (((0,), (0,)), ((), ())), preferred_element_type=jnp.float32
@@ -260,10 +270,11 @@
             pltpu.VMEM((count, LANES), f32),
             pltpu.VMEM((rows, count), f32),
             pltpu.VMEM((rows, count), f32),
+            pltpu.VMEM((rows, count), f32),
             pltpu.VMEM((rows, count), bf16),
             pltpu.VMEM((n, 2 * own, width), f32),
-            pltpu.VMEM((n, 2, rows), f32),
-            pltpu.VMEM((n, 2, rows), f32),
+            pltpu.VMEM((n, 1, rows), f32),
+            pltpu.VMEM((n, 3, rows), f32),
             pltpu.VMEM((n, own, width), f32),
             pltpu.VMEM((n, own, width), f32),
             pltpu.VMEM((rows, width), bf16),

time: 40.2 us -> 37.3 us (0.928)
  Pallas kernels: 36.2 us -> 33.3 us
    pallas_call x1, Pallas kernels: 36.2 us -> 33.3 us  [body(): pl.pallas_call(functools.partial(kernel, dp, proto, cols), out_shape=(jax...]
where the time goes in v3:
time: 37.3 us; the launch traced here: 37.1 us
  Pallas kernels  33.3 us (89%)
  local copies, waits for them, and re-layouts  3.13 us (8%)
  between operations  0.66 us (2%)
    pallas_call x1, Pallas kernels, body(): pl.pallas_call(functools.partial(kernel, dp, proto, cols), out_shape=(jax...  33.3 us
    unnamed x7, local copies, waits for them, and re-layouts  3.13 us

profile of v3, /device:TPU:0, one launch (start us, length us, event | category | flops | bytes accessed | tf_op | source)
XLA Modules:
  0.0 37.1 jit_solution(8542718829330841415)
XLA Ops:
  0.6 33.3 %shard_map.67 = (f32[1,4]{1,0:T(1,128)}, f32[4,256]{1,0:T(4,128)}, f32[4096,256]{1,0:T(8,128)S(1)}) custom-call(bf16[4,256]{1,0:T(4,128)(2,1)} %t_ref.1, bf16[4,256]{1,0:T(4,128)(2,1)} %s_ref.1, bf16[4096,256]{1,0:T(8,128)(2,1)} %tw_hbm.1, bf16[4096,256]{1,0:T(8,128)(2,1)} %sw_hbm.1), custom_call_target="tpu_custom_call" | custom-call | tf_op jit(solution)/shard_map/pallas_call | solution.py:256
  34.0 0.0 copy-start.1
  34.0 0.0 copy-start
  34.0 2.0 %copy.10 = f32[4096,256]{1,0:T(8,128)} copy(f32[4096,256]{1,0:T(8,128)S(1)} %get-tuple-element.11) | data formatting | bytes 8388608
  36.0 0.0 copy-done.1
  36.0 0.5 %copy.11 = f32[4]{0:T(128)} copy(f32[4]{0:T(128)S(1)} %bitcast.1) | data formatting | bytes 32
  36.5 0.0 copy-done
  36.5 0.6 %copy.12 = f32[4,256]{1,0:T(4,128)} copy(f32[4,256]{1,0:T(4,128)S(1)} %copy-done) | data formatting | bytes 8192
Async XLA Ops:
  34.0 2.0 %copy-start.1 = (f32[1,4]{1,0:T(1,128)S(1)}, f32[1,4]{1,0:T(1,128)}, u32[]{:S(2)}) copy-start(f32[1,4]{1,0:T(1,128)} %get-tuple-element.6) | copy-start | bytes 52
  34.0 2.5 %copy-start = (f32[4,256]{1,0:T(4,128)S(1)}, f32[4,256]{1,0:T(4,128)}, u32[]{:S(2)}) copy-start(f32[4,256]{1,0:T(4,128)} %get-tuple-element.16) | copy-start | bytes 12292

commit v4 on v3

--- a/solution.py
+++ b/solution.py
@@ -16,6 +16,13 @@
 LOAD_PARTS = 4
 
 
+def inner_size(n):
+    size = 1
+    while n % (2 * size) == 0 and 2 * size * size <= n:
+        size *= 2
+    return size
+
+
 def inverse_norm(x):
     return lax.rsqrt(jnp.sum(x * x, axis=-1, keepdims=True) + EPSILON)
 
@@ -66,7 +73,7 @@
     t_ref, s_ref, tw_hbm, sw_hbm,
     loss_ref, sgrad_ref, pgrad_ref,
     tw_raw, sw_raw, tw_unit, sw_unit, sw_inv, texp, logit, sexp, delta,
-    rows_buf, sums1, sums2, part, landed, t_all, s_all,
+    rows_buf, sums1, again1, sums2, again2, part, landed, passed, summed, t_all, s_all,
     load_sem, send_sem, recv_sem,
 ):
     n = dp * proto
@@ -77,14 +84,20 @@
     chunks = count // cols
     me = lax.axis_index("dp") * proto + lax.axis_index("proto")
 
-    def coords(j):
-        peer = lax.rem(me + j, n)
-        return peer, (lax.div(peer, proto), lax.rem(peer, proto))
+    inner = inner_size(n)
+    outer = n // inner
+    low, high = lax.rem(me, inner), lax.div(me, inner)
+    sizes, places = (inner, outer), (low, high)
+
+    def neighbour(stage, j):
+        place = lax.rem(places[stage] + j, sizes[stage])
+        peer = high * inner + place if stage == 0 else place * inner + low
+        return place, (lax.div(peer, proto), lax.rem(peer, proto))
 
     piece = count // LOAD_PARTS
     loads = []
-    for k in range(LOAD_PARTS):
-        for index, (hbm, raw) in enumerate(((tw_hbm, tw_raw), (sw_hbm, sw_raw))):
+    for index, (hbm, raw) in enumerate(((tw_hbm, tw_raw), (sw_hbm, sw_raw))):
+        for k in range(LOAD_PARTS):
             span = pl.ds(k * piece, piece)
             copy = pltpu.make_async_copy(hbm.at[span], raw.at[span], load_sem.at[index, k])
             copy.start()
@@ -92,42 +105,49 @@
 
     barrier = pltpu.get_barrier_semaphore()
 
-    @pl.loop(1, n)
-    def _(j):
-        pl.semaphore_signal(barrier, inc=1, device_id=coords(j)[1], device_id_type=pl.DeviceIdType.MESH)
+    for stage in range(2):
+        for j in range(1, sizes[stage]):
+            pl.semaphore_signal(
+                barrier, inc=1, device_id=neighbour(stage, j)[1], device_id_type=pl.DeviceIdType.MESH
+            )
 
     t_own = t_ref[...].astype(jnp.float32)
     s_own = s_ref[...].astype(jnp.float32)
     s_own_inv = inverse_norm(s_own)
     t_rounded = (t_own * inverse_norm(t_own)).astype(jnp.bfloat16).astype(jnp.float32)
     s_rounded = (s_own * s_own_inv).astype(jnp.bfloat16).astype(jnp.float32)
-    rows_buf[me] = jnp.concatenate([t_rounded, s_rounded], axis=0)
-    pl.semaphore_wait(barrier, n - 1)
-
-    def spread(phase, source, target):
-        @pl.loop(1, n)
-        def _(j):
-            peer, device = coords(j)
+    rows_buf[high, low] = jnp.concatenate([t_rounded, s_rounded], axis=0)
+    pl.semaphore_wait(barrier, inner + outer - 2)
+
+    def spread(phase, stage, source, target):
+        for j in range(1, sizes[stage]):
+            place, device = neighbour(stage, j)
             pltpu.make_async_remote_copy(
-                src_ref=source(peer), dst_ref=target.at[me],
-                send_sem=send_sem.at[phase], recv_sem=recv_sem.at[phase],
+                src_ref=source(place), dst_ref=target,
+                send_sem=send_sem.at[phase, stage], recv_sem=recv_sem.at[phase, stage],
                 device_id=device, device_id_type=pl.DeviceIdType.MESH,
             ).start()
 
-    def whole(phase, target):
-        span = pl.ds(0, n - 1)
+    def whole(phase, stage, view):
         return pltpu.make_async_remote_copy(
-            src_ref=target.at[span], dst_ref=target.at[span],
-            send_sem=send_sem.at[phase], recv_sem=recv_sem.at[phase],
-            device_id=coords(1)[1], device_id_type=pl.DeviceIdType.MESH,
+            src_ref=view, dst_ref=view,
+            send_sem=send_sem.at[phase, stage], recv_sem=recv_sem.at[phase, stage],
+            device_id=neighbour(stage, 1)[1], device_id_type=pl.DeviceIdType.MESH,
         )
 
-    spread(0, lambda peer: rows_buf.at[me], rows_buf)
+    def others(stage, buffer):
+        return buffer.at[pl.ds(0, sizes[stage] - 1)]
+
+    block_rows = rows_buf.at[high]
+    spread(0, 0, lambda place: block_rows.at[low], block_rows.at[low])
 
     norm_rows = min(piece, 512)
-    for k in range(LOAD_PARTS):
-        for index, raw in enumerate((tw_raw, sw_raw)):
-            loads[2 * k + index].wait()
+    for index, raw in enumerate((tw_raw, sw_raw)):
+        if index == 1:
+            whole(0, 0, others(0, block_rows)).wait_recv()
+            spread(0, 1, lambda place: block_rows, block_rows)
+        for k in range(LOAD_PARTS):
+            loads[index * LOAD_PARTS + k].wait()
 
             @pl.loop(0, piece // norm_rows)
             def _(c, k=k, index=index, raw=raw):
@@ -141,7 +161,7 @@
                     sw_unit[span] = unit
                     sw_inv[span] = inverse
 
-    whole(0, rows_buf).wait_recv()
+    whole(0, 1, others(1, rows_buf)).wait_recv()
     paired = rows_buf[...].reshape(n // 2, 2, 2 * own, width)
     first, second = paired[:, 0], paired[:, 1]
     upper = lax.broadcasted_iota(jnp.int32, first.shape, 1) < own
@@ -154,8 +174,10 @@
     def span_of(c):
         return pl.ds(c * cols, cols)
 
-    def over_chunks(step, carry):
-        for c in range(chunks):
+    half = (chunks + 1) // 2
+
+    def over_chunks(step, carry, first=0, last=chunks):
+        for c in range(first, last):
             carry = step(c, carry)
         return carry
 
@@ -181,16 +203,23 @@
 
     def send_sums(phase, sums, parts):
         rows = [to_lanes(jnp.sum(x, axis=1, keepdims=True)) for x in parts]
-        sums[me] = rows[0] if len(rows) == 1 else jnp.concatenate(rows, axis=0)
-        spread(phase, lambda peer: sums.at[me], sums)
-
-    def receive_sums(phase, sums):
-        whole(phase, sums).wait_recv()
-        return jnp.sum(sums[...], axis=0)
+        sums[low] = rows[0] if len(rows) == 1 else jnp.concatenate(rows, axis=0)
+        spread(phase, 0, lambda place: sums.at[low], sums.at[low])
+
+    def pass_on(phase, sums, again):
+        whole(phase, 0, others(0, sums)).wait_recv()
+        again[high] = jnp.sum(sums[...], axis=0)
+        spread(phase, 1, lambda place: again.at[high], again.at[high])
+
+    def receive_sums(phase, again):
+        whole(phase, 1, others(1, again)).wait_recv()
+        return jnp.sum(again[...], axis=0)
 
     send_sums(1, sums1, (over_chunks(first_pass, zeros),))
-    exp_sum = over_chunks(student_pass, zeros)
-    row_total = receive_sums(1, sums1)
+    exp_sum = over_chunks(student_pass, zeros, 0, half)
+    pass_on(1, sums1, again1)
+    exp_sum = over_chunks(student_pass, exp_sum, half, chunks)
+    row_total = receive_sums(1, again1)
     row_scale = to_column(1.0 / row_total)
 
     def second_pass(c, carry):
@@ -204,7 +233,8 @@
 
     row_sum, dot_sum = over_chunks(second_pass, (zeros, zeros))
     send_sums(2, sums2, (row_sum, dot_sum, exp_sum))
-    total = receive_sums(2, sums2)
+    pass_on(2, sums2, again2)
+    total = receive_sums(2, again2)
     row_total, dot_total, exp_total = total[0:1], total[1:2], total[2:3]
     factor = LOSS_SCALE / STUD_TEMP
     row_scale = to_column(factor / row_total)
@@ -217,16 +247,18 @@
         return carry + jnp.dot(gradient, sw_unit[span], preferred_element_type=jnp.float32)
 
     row_part = over_chunks(third_pass, jnp.zeros((total_rows, width), jnp.float32))
-    part[...] = row_part.reshape(n, own, width)
-    landed[me] = part[me]
-    spread(3, lambda peer: part.at[peer], landed)
+    blocks = row_part.reshape(outer, inner, own, width)
+    for h in range(outer):
+        part[:, h] = blocks[h]
+    landed[low] = part[low]
+    spread(3, 0, lambda place: part.at[place], landed.at[low])
 
     loss = jnp.log(exp_total) - dot_total / row_total
     shape = (total_rows, LANES)
     mine = lax.broadcasted_iota(jnp.int32, shape, 0) == me * own + lax.broadcasted_iota(jnp.int32, shape, 1)
     loss_ref[...] = jnp.sum(jnp.where(mine, to_column(loss), 0.0), axis=0, keepdims=True)[:, :own]
 
-    for c in range(chunks):
+    def grad_pass(c, carry):
         span = span_of(c)
         g = lax.dot_general(
             delta[:, span], s_all[...], (((0,), (0,)), ((), ())), preferred_element_type=jnp.float32
@@ -235,17 +267,28 @@
         inverse = sw_inv[span]
         pull = (inverse * inverse * inverse) * sum_wide(x * g)
         pgrad_ref[span] = widen(inverse, width) * g - x * widen(pull, width)
-
-    whole(3, landed).wait_recv()
-    g = jnp.sum(landed[...], axis=0)
+        return carry
+
+    over_chunks(grad_pass, 0, 0, half)
+    whole(3, 0, others(0, landed)).wait_recv()
+    passed[...] = jnp.sum(landed[...], axis=0)
+    summed[high] = passed[high]
+    spread(3, 1, lambda place: passed.at[place], summed.at[high])
+    over_chunks(grad_pass, 0, half, chunks)
+    whole(3, 1, others(1, summed)).wait_recv()
+    g = jnp.sum(summed[...], axis=0)
     projected = jnp.sum(s_own * g, axis=1, keepdims=True)
     sgrad_ref[...] = s_own_inv * g - s_own * (s_own_inv * s_own_inv * s_own_inv) * projected
-    for phase, target in enumerate((rows_buf, sums1, sums2, landed)):
-        whole(phase, target).wait_send()
+    pairs = ((block_rows, rows_buf), (sums1, again1), (sums2, again2), (landed, summed))
+    for phase, pair in enumerate(pairs):
+        for stage, buffer in enumerate(pair):
+            whole(phase, stage, others(stage, buffer)).wait_send()
 
 
 def body(dp, proto, teacher_rows, student_rows, teacher_protos, student_protos):
     n = dp * proto
+    inner = inner_size(n)
+    outer = n // inner
     own, width = teacher_rows.shape
     count = teacher_protos.shape[0]
     rows = n * own
@@ -272,16 +315,20 @@
             pltpu.VMEM((rows, count), f32),
             pltpu.VMEM((rows, count), f32),
             pltpu.VMEM((rows, count), bf16),
-            pltpu.VMEM((n, 2 * own, width), f32),
-            pltpu.VMEM((n, 1, rows), f32),
-            pltpu.VMEM((n, 3, rows), f32),
-            pltpu.VMEM((n, own, width), f32),
-            pltpu.VMEM((n, own, width), f32),
+            pltpu.VMEM((outer, inner, 2 * own, width), f32),
+            pltpu.VMEM((inner, 1, rows), f32),
+            pltpu.VMEM((outer, 1, rows), f32),
+            pltpu.VMEM((inner, 3, rows), f32),
+            pltpu.VMEM((outer, 3, rows), f32),
+            pltpu.VMEM((inner, outer, own, width), f32),
+            pltpu.VMEM((inner, outer, own, width), f32),
+            pltpu.VMEM((outer, own, width), f32),
+            pltpu.VMEM((outer, own, width), f32),
             pltpu.VMEM((rows, width), bf16),
             pltpu.VMEM((rows, width), bf16),
             pltpu.SemaphoreType.DMA((2, LOAD_PARTS)),
-            pltpu.SemaphoreType.DMA((4,)),
-            pltpu.SemaphoreType.DMA((4,)),
+            pltpu.SemaphoreType.DMA((4, 2)),
+            pltpu.SemaphoreType.DMA((4, 2)),
         ],
         compiler_params=pltpu.CompilerParams(
             collective_id=0, has_side_effects=True, vmem_limit_bytes=56 * 1024 * 1024

time: 37.3 us -> 44.6 us (1.20)
  Pallas kernels: 33.3 us -> 40.6 us
    pallas_call x1, Pallas kernels: 33.3 us -> 40.6 us  [body(): pl.pallas_call(functools.partial(kernel, dp, proto, cols), out_shape=(jax...]
where the time goes in v4:
time: 44.6 us; the launch traced here: 44.4 us
  Pallas kernels  40.6 us (91%)
  local copies, waits for them, and re-layouts  3.13 us (7%)
  between operations  0.66 us (1%)
    pallas_call x1, Pallas kernels, body(): pl.pallas_call(functools.partial(kernel, dp, proto, cols), out_shape=(jax...  40.6 us
    unnamed x7, local copies, waits for them, and re-layouts  3.13 us

profile of v4, /device:TPU:0, one launch (start us, length us, event | category | flops | bytes accessed | tf_op | source)
XLA Modules:
  0.0 44.4 jit_solution(2955951323616098031)
XLA Ops:
  0.6 40.6 %shard_map.67 = (f32[1,4]{1,0:T(1,128)}, f32[4,256]{1,0:T(4,128)}, f32[4096,256]{1,0:T(8,128)S(1)}) custom-call(bf16[4,256]{1,0:T(4,128)(2,1)} %t_ref.1, bf16[4,256]{1,0:T(4,128)(2,1)} %s_ref.1, bf16[4096,256]{1,0:T(8,128)(2,1)} %tw_hbm.1, bf16[4096,256]{1,0:T(8,128)(2,1)} %sw_hbm.1), custom_call_target="tpu_custom_call" | custom-call | tf_op jit(solution)/shard_map/pallas_call | solution.py:299
  41.3 0.0 copy-start.1
  41.3 0.0 copy-start
  41.3 2.0 %copy.10 = f32[4096,256]{1,0:T(8,128)} copy(f32[4096,256]{1,0:T(8,128)S(1)} %get-tuple-element.11) | data formatting | bytes 8388608
  43.3 0.0 copy-done.1
  43.3 0.5 %copy.11 = f32[4]{0:T(128)} copy(f32[4]{0:T(128)S(1)} %bitcast.1) | data formatting | bytes 32
  43.8 0.0 copy-done
  43.8 0.6 %copy.12 = f32[4,256]{1,0:T(4,128)} copy(f32[4,256]{1,0:T(4,128)S(1)} %copy-done) | data formatting | bytes 8192
Async XLA Ops:
  41.3 2.0 %copy-start.1 = (f32[1,4]{1,0:T(1,128)S(1)}, f32[1,4]{1,0:T(1,128)}, u32[]{:S(2)}) copy-start(f32[1,4]{1,0:T(1,128)} %get-tuple-element.6) | copy-start | bytes 52
  41.3 2.5 %copy-start = (f32[4,256]{1,0:T(4,128)S(1)}, f32[4,256]{1,0:T(4,128)}, u32[]{:S(2)}) copy-start(f32[4,256]{1,0:T(4,128)} %get-tuple-element.16) | copy-start | bytes 12292

commit v5 on v3

--- a/solution.py
+++ b/solution.py
@@ -83,8 +83,8 @@
 
     piece = count // LOAD_PARTS
     loads = []
-    for k in range(LOAD_PARTS):
-        for index, (hbm, raw) in enumerate(((tw_hbm, tw_raw), (sw_hbm, sw_raw))):
+    for index, (hbm, raw) in enumerate(((tw_hbm, tw_raw), (sw_hbm, sw_raw))):
+        for k in range(LOAD_PARTS):
             span = pl.ds(k * piece, piece)
             copy = pltpu.make_async_copy(hbm.at[span], raw.at[span], load_sem.at[index, k])
             copy.start()
@@ -102,8 +102,6 @@
     t_rounded = (t_own * inverse_norm(t_own)).astype(jnp.bfloat16).astype(jnp.float32)
     s_rounded = (s_own * s_own_inv).astype(jnp.bfloat16).astype(jnp.float32)
     rows_buf[me] = jnp.concatenate([t_rounded, s_rounded], axis=0)
-    pl.semaphore_wait(barrier, n - 1)
-
     def spread(phase, source, target):
         @pl.loop(1, n)
         def _(j):
@@ -122,12 +120,13 @@
             device_id=coords(1)[1], device_id_type=pl.DeviceIdType.MESH,
         )
 
-    spread(0, lambda peer: rows_buf.at[me], rows_buf)
-
     norm_rows = min(piece, 512)
-    for k in range(LOAD_PARTS):
-        for index, raw in enumerate((tw_raw, sw_raw)):
-            loads[2 * k + index].wait()
+    for index, raw in enumerate((tw_raw, sw_raw)):
+        if index == 1:
+            pl.semaphore_wait(barrier, n - 1)
+            spread(0, lambda peer: rows_buf.at[me], rows_buf)
+        for k in range(LOAD_PARTS):
+            loads[index * LOAD_PARTS + k].wait()
 
             @pl.loop(0, piece // norm_rows)
             def _(c, k=k, index=index, raw=raw):

time: 37.3 us -> 37.3 us (level)
  no operation moved by 1% of the time
where the time goes in v5:
time: 37.3 us; the launch traced here: 37.1 us
  Pallas kernels  33.3 us (89%)
  local copies, waits for them, and re-layouts  3.13 us (8%)
  between operations  0.66 us (2%)
    pallas_call x1, Pallas kernels, body(): pl.pallas_call(functools.partial(kernel, dp, proto, cols), out_shape=(jax...  33.3 us
    unnamed x7, local copies, waits for them, and re-layouts  3.13 us

profile of v5, /device:TPU:0, one launch (start us, length us, event | category | flops | bytes accessed | tf_op | source)
XLA Modules:
  0.0 37.1 jit_solution(16240365607916037967)
XLA Ops:
  0.6 33.3 %shard_map.67 = (f32[1,4]{1,0:T(1,128)}, f32[4,256]{1,0:T(4,128)}, f32[4096,256]{1,0:T(8,128)S(1)}) custom-call(bf16[4,256]{1,0:T(4,128)(2,1)} %t_ref.1, bf16[4,256]{1,0:T(4,128)(2,1)} %s_ref.1, bf16[4096,256]{1,0:T(8,128)(2,1)} %tw_hbm.1, bf16[4096,256]{1,0:T(8,128)(2,1)} %sw_hbm.1), custom_call_target="tpu_custom_call" | custom-call | tf_op jit(solution)/shard_map/pallas_call | solution.py:255
  34.0 0.0 copy-start.1
  34.0 0.0 copy-start
  34.0 2.0 %copy.10 = f32[4096,256]{1,0:T(8,128)} copy(f32[4096,256]{1,0:T(8,128)S(1)} %get-tuple-element.11) | data formatting | bytes 8388608
  36.0 0.0 copy-done.1
  36.0 0.5 %copy.11 = f32[4]{0:T(128)} copy(f32[4]{0:T(128)S(1)} %bitcast.1) | data formatting | bytes 32
  36.5 0.0 copy-done
  36.5 0.6 %copy.12 = f32[4,256]{1,0:T(4,128)} copy(f32[4,256]{1,0:T(4,128)S(1)} %copy-done) | data formatting | bytes 8192
Async XLA Ops:
  34.0 2.0 %copy-start.1 = (f32[1,4]{1,0:T(1,128)S(1)}, f32[1,4]{1,0:T(1,128)}, u32[]{:S(2)}) copy-start(f32[1,4]{1,0:T(1,128)} %get-tuple-element.6) | copy-start | bytes 52
  34.0 2.5 %copy-start = (f32[4,256]{1,0:T(4,128)S(1)}, f32[4,256]{1,0:T(4,128)}, u32[]{:S(2)}) copy-start(f32[4,256]{1,0:T(4,128)} %get-tuple-element.16) | copy-start | bytes 12292
